TPU v7x, 32 devices: a whole 2x2x4 slice. The times are simulated.
32 devices in a mesh: exp: 8 (over z, y), row: 4 (over x, core).
Axes of the slice: x: 2, y: 2, z: 4, core: 2. Of those that a mesh axis runs over, the one named last changes fastest.
Arguments:
- latent: bfloat16 [4, 1024, 1024], P(None, 'row', 'exp'), may hold values from -6 to 6
- row_taps: bfloat16 [16, 21], replicated, may hold values from -1.25 to 1.25
- column_taps: bfloat16 [16, 21], replicated, may hold values from -1.25 to 1.25
- coefficients: bfloat16 [8, 16, 1024, 1024], P('exp', None, 'row'), may hold values from -1.5 to 1.5
- observed: bfloat16 [8, 1024, 1024], P('exp', 'row'), may hold values from -6 to 6
- cell_of: int32 [8, 1], replicated, may hold values from 0 to 3
- valid_rows: int32 [8, 1024], P('exp', 'row'), may hold values 0 or 1
Outputs:
- gradient: float32 [4, 1024, 1024], P(None, 'row', 'exp')
- residuals: float32 [8, 1024, 1024], P('exp', 'row')
Inputs may be any that keep to these rules, and one draw needn't show every extreme that they name: `cell_of`: every sky cell is covered by at least one exposure.
All inputs are finite; a program needn't handle non-finite values. No bound on the sum of `valid_rows` on one device may be relied on, other than what follows from the above.
Results may differ from a plain program's by a relative error of at most 0.0023.
Values may be sent and summed in bfloat16 or wider, within the bound.
A program may use at most 128 MiB of HBM per device.

v0:
```python
import jax
import jax.numpy as jnp
from jax import lax
from jax.sharding import PartitionSpec as P


def padded_2(cells, sides, width):
    for axis, dim in sides:
        count = lax.axis_size(axis)
        ends = count - 1
        head = lax.slice_in_dim(cells, 0, width, axis=dim)
        tail = lax.slice_in_dim(cells, cells.shape[dim] - width, cells.shape[dim], axis=dim)
        cells = jnp.concatenate(
            [
                lax.ppermute(tail, axis, [(i, (i + 1) % count) for i in range(ends)]),
                cells,
                lax.ppermute(head, axis, [((i + 1) % count, i) for i in range(ends)]),
            ],
            axis=dim,
        )
    return cells


def from_behind(block, axis, distance):
    devices = range(lax.axis_size(axis))
    route = [(i - distance, i) for i in devices if i - distance in devices]
    return lax.ppermute(block, axis, route)


def bands(kernel_taps, adjoint):
    tap_count = kernel_taps.shape[1]
    halfwidth = tap_count // 2
    inputs_at = lax.broadcasted_iota(jnp.int32, (384, 128), 0)
    outputs_at = lax.broadcasted_iota(jnp.int32, (384, 128), 1)
    if adjoint:
        offset = outputs_at - inputs_at + 128 + halfwidth
    else:
        offset = inputs_at - 128 - outputs_at + halfwidth
    onehot = (offset[:, :, None] == jnp.arange(tap_count)[None, None, :]).astype(jnp.float32)
    return jnp.einsum("kt,pqt->kpq", kernel_taps.astype(jnp.float32), onehot).astype(jnp.bfloat16)


def column_matrix(kernel_taps, strip_rows):
    tap_count = kernel_taps.shape[1]
    halfwidth = tap_count // 2
    outputs_at = lax.broadcasted_iota(jnp.int32, (strip_rows, strip_rows + 2 * halfwidth), 0)
    inputs_at = lax.broadcasted_iota(jnp.int32, (strip_rows, strip_rows + 2 * halfwidth), 1)
    offset = inputs_at - outputs_at
    onehot = (offset[:, :, None] == jnp.arange(tap_count)[None, None, :]).astype(jnp.float32)
    return jnp.einsum("kt,yit->kyi", kernel_taps.astype(jnp.float32), onehot).astype(jnp.bfloat16)


def stacked_blocks(source):
    length = source.shape[-1]
    nblocks = length // 128
    padding = [(0, 0)] * (source.ndim - 1) + [(128, 128)]
    padded = jnp.pad(source, padding)
    blocked = padded.reshape(source.shape[:-1] + (nblocks + 2, 128))
    return jnp.concatenate(
        [blocked[..., :-2, :], blocked[..., 1:-1, :], blocked[..., 2:, :]], axis=-1
    )


def body(latent, row_taps, column_taps, coefficients, observed, cell_of, valid_rows):
    tap_count = row_taps.shape[1]
    halfwidth = tap_count // 2
    kernel_count = row_taps.shape[0]
    strip_rows = observed.shape[1]
    cell_width = observed.shape[2]
    ncells = latent.shape[0]
    cell_list = cell_of[:, 0]
    outgoing = jnp.take(latent, cell_list, axis=0)
    arrived = lax.all_to_all(outgoing, "exp", split_axis=0, concat_axis=2, tiled=True)
    cell_strip = arrived[0]
    extended = padded_2(cell_strip, (("row", 0),), halfwidth)
    rowblur = jnp.einsum(
        "rbp,kpq->krbq",
        stacked_blocks(extended),
        bands(row_taps, False),
        preferred_element_type=jnp.float32,
    )
    rowblur = rowblur.reshape(kernel_count, strip_rows + 2 * halfwidth, cell_width).astype(
        jnp.bfloat16
    )
    matrix = column_matrix(column_taps, strip_rows)
    vertical = jnp.einsum("kyi,kix->kyx", matrix, rowblur, preferred_element_type=jnp.float32)
    coeffs = coefficients[0].astype(jnp.float32)
    predicted = jnp.sum(coeffs * vertical, axis=0)
    row_mask = valid_rows[0].astype(jnp.float32)[:, None]
    residual = row_mask * (predicted - observed[0].astype(jnp.float32))
    weighted = (coeffs * residual[None]).astype(jnp.bfloat16)
    colback_ext = jnp.einsum("kyi,kyx->kix", matrix, weighted, preferred_element_type=jnp.float32)
    upper_rim = colback_ext[:, :halfwidth]
    lower_rim = colback_ext[:, strip_rows + halfwidth :]
    from_below = from_behind(upper_rim.astype(jnp.bfloat16), "row", -1).astype(upper_rim.dtype)
    from_above = from_behind(lower_rim.astype(jnp.bfloat16), "row", 1).astype(lower_rim.dtype)
    middle = colback_ext[:, halfwidth : strip_rows + halfwidth]
    middle = middle.at[:, :halfwidth].add(from_above)
    middle = middle.at[:, strip_rows - halfwidth :].add(from_below)
    colback = middle.astype(jnp.bfloat16)
    own_term = jnp.einsum(
        "krbp,kpq->rbq",
        stacked_blocks(colback),
        bands(row_taps, True),
        preferred_element_type=jnp.float32,
    ).reshape(strip_rows, cell_width)
    incoming = lax.all_to_all(own_term[None], "exp", split_axis=2, concat_axis=0, tiled=True)
    owner_table = (jnp.arange(ncells)[:, None] == cell_list[None, :]).astype(jnp.float32)
    gradient = jnp.einsum("cn,nrw->crw", owner_table, incoming, precision=lax.Precision.HIGHEST)
    return (gradient, residual[None])


def solution(mesh):
    placed = (
        P(None, "row", "exp"),
        P(),
        P(),
        P("exp", None, "row", None),
        P("exp", "row", None),
        P(),
        P("exp", "row"),
    )
    return jax.shard_map(
        body,
        mesh=mesh,
        in_specs=placed,
        out_specs=(P(None, "row", "exp"), P("exp", "row", None)),
        check_vma=False,
    )
```

profile of v0, /device:TPU:0, one launch (start us, length us, event | category | flops | bytes accessed | tf_op | source)
XLA Modules:
  0.0 269.2 jit_solution(5285161307771995136)
XLA Ops:
  3.6 7.3 %all-to-all-start = ((bf16[8,256,128]{2,1,0:T(8,128)(2,1)}), bf16[8,256,128]{2,1,0:T(8,128)(2,1)S(1)}, u32[]{:S(2)}, u32[]{:S(2)}) async-start(bf16[8,256,128]{2,1,0:T(8,128)(2,1)} %broadcast_select_fusion), calls=%async_computation | async-start | bytes 1048576 | tf_op jit(solution)/shard_map/all_to_all | solution.py:73
  11.0 2.2 convert_bitcast_fusion.1
  13.2 12.1 %all-to-all-done = bf16[8,256,128]{2,1,0:T(8,128)(2,1)S(1)} async-done(((bf16[8,256,128]{2,1,0:T(8,128)(2,1)}), bf16[8,256,128]{2,1,0:T(8,128)(2,1)S(1)}, u32[]{:S(2)}, u32[]{:S(2)}) %all-to-all-start) | async-done | bytes 524320 | tf_op jit(solution)/shard_map/all_to_all | solution.py:73
  25.6 1.3 collective-permute-start.1
  26.9 3.0 %collective-permute-start = (bf16[10,1024]{1,0:T(8,128)(2,1)S(1)}, bf16[10,1024]{1,0:T(8,128)(2,1)S(1)}, u32[]{:S(2)}, u32[]{:S(2)}) collective-permute-start(bf16[10,1024]{1,0:T(8,128)(2,1)S(1)} %bitcast.84), channel_id=1, source_target_pairs={{0,1},{1,2},{2,3},{4,5},{5,6},{6,7},{8,9},{9,10},{10,11},{12,13},{... | collective-permute-start | bytes 61448 | tf_op jit(solution)/shard_map/ppermute | solution.py:15
  30.0 3.0 %fusion.29 = bf16[16,384,128,1]{2,0,1,3:T(8,128)(2,1)} fusion(s32[384,128]{1,0:T(8,128)S(1)} %subtract_add_fusion.1, bf16[16,21]{1,0:T(8,128)(2,1)} %param.12), kind=kOutput, calls=%fused_computation.39 | convolution fusion | flops 34848768 | bytes 1770144 | tf_op jit(solution)/shard_map/kt,pqt->kpq/dot_general | solution.py:40
  34.2 1.6 fusion.38
  35.8 1.5 fusion.50
  37.3 2.2 copy.91
  39.5 2.2 copy.92
  42.8 10.3 %convert_bitcast_fusion = bf16[16,276,8,128]{3,1,2,0:T(8,128)(2,1)} fusion(bf16[276,8,128]{2,0,1:T(8,128)(2,1)} %copy.93, bf16[276,8,128]{2,0,1:T(8,128)(2,1)} %copy.92, bf16[276,8,128]{2,0,1:T(8,128)(2,1)} %copy.91, bf16[16,384,128,1]{2,0,1,3:T(8,128)(2,1)} %fusion.29), kind=kOutput, calls=%fused_computation.11 | convolution fusion | flops 3482492928 | bytes 12312576 | tf_op jit(solution)/shard_map/rbp,kpq->krbq/dot_general | solution.py:76
  53.2 8.3 %copy.86 = bf16[16,276,8,128]{3,2,1,0:T(8,128)(2,1)} copy(bf16[16,276,8,128]{3,1,2,0:T(8,128)(2,1)} %convert_bitcast_fusion) | data formatting | bytes 18087936 | tf_op jit(solution)/shard_map/convert_element_type | solution.py:82
  61.5 14.0 %reshape.150 = bf16[16,276,1024]{2,1,0:T(8,128)(2,1)} reshape(bf16[16,276,8,128]{3,2,1,0:T(8,128)(2,1)} %copy.86) | data formatting | bytes 18087936 | tf_op jit(solution)/shard_map/convert_element_type | solution.py:82
  75.5 12.3 %fusion.6 = f32[256,1024]{1,0:T(8,128)S(1)} fusion(bf16[16,276,1024]{2,1,0:T(8,128)(2,1)} %reshape.150, bf16[1,16,256,1024]{3,2,1,0:T(8,128)(2,1)} %param.14, bf16[16,256,276]{1,0,2:T(8,128)(2,1)S(1)} %convert_bitcast_fusion.1), kind=kOutput, calls=%fused_computation.9 | convolution fusion | flops 2327576576 | bytes 20742144 | tf_op jit(solution)/shard_map/kyi,kix->kyx/dot_general | solution.py:86
  89.0 16.5 %fusion.52 = (bf16[16,276,1024]{2,1,0:T(8,128)(2,1)}, f32[16,276,1024]{2,1,0:T(8,128)}) fusion(bf16[1,16,256,1024]{3,2,1,0:T(8,128)(2,1)} %param.14, f32[256,1024]{1,0:T(8,128)} %bitcast.75, bf16[16,256,276]{1,0,2:T(8,128)(2,1)S(1)} %convert_bitcast_fusion.1), kind=kOutput, calls=%fused_computation.74 | convolution fusion | flops 2332360704 | bytes 38830080 | tf_op jit(solution)/shard_map/kyi,kyx->kix/dot_general | solution.py:92
  105.5 2.4 fusion.49
  107.9 3.8 %collective-permute-start.2 = (bf16[16,10,1024]{2,1,0:T(8,128)(2,1)}, bf16[16,10,1024]{2,1,0:T(8,128)(2,1)}, u32[]{:S(2)}, u32[]{:S(2)}) collective-permute-start(bf16[16,10,1024]{2,1,0:T(8,128)(2,1)} %get-tuple-element.38), channel_id=1, source_target_pairs={{0,1},{1,2},{2,3},{4,5},{5,6},{6,7},{8,9},{9,10},{10,11},{12,13},{... | collective-permute-start | bytes 983048 | tf_op jit(solution)/shard_map/ppermute | solution.py:27
  114.1 1.5 copy.73
  115.6 12.6 %slice.112 = f32[16,256,1024]{2,1,0:T(8,128)} slice(f32[16,276,1024]{2,1,0:T(8,128)} %get-tuple-element.45), slice={[0:16], [10:266], [0:1024]} | slice | bytes 33554432 | tf_op jit(solution)/shard_map/slice | solution.py:97
  128.2 1.7 slice_add_fusion.1
  129.9 5.9 %scatter-add.6 = f32[16,256,1024]{2,1,0:T(8,128)} dynamic-update-slice(f32[16,256,1024]{2,1,0:T(8,128)} %slice.112, f32[16,10,1024]{2,1,0:T(8,128)S(1)} %slice_add_fusion.1, s32[]{:T(128)} %constant.74.clone.1, s32[]{:T(128)} %constant.74.clone.1, s32[]{:T(128)} %constant.74.clone.1) | dynamic-update-slice | bytes 1310724 | tf_op jit(solution)/shard_map/scatter-add | solution.py:98
  135.9 1.5 slice_add_fusion
  137.4 5.1 %scatter-add.9 = f32[16,256,1024]{2,1,0:T(8,128)} dynamic-update-slice(f32[16,256,1024]{2,1,0:T(8,128)} %scatter-add.6, f32[16,10,1024]{2,1,0:T(8,128)S(1)} %slice_add_fusion, s32[]{:T(128)} %constant.74.clone.1, s32[]{:T(128)} %constant.80.clone.1, s32[]{:T(128)} %constant.74.clone.1) | dynamic-update-slice | bytes 1310724 | tf_op jit(solution)/shard_map/scatter-add | solution.py:99
  142.5 9.1 %convert_element_type.87 = bf16[16,256,1024]{2,1,0:T(8,128)(2,1)} convert(f32[16,256,1024]{2,1,0:T(8,128)} %scatter-add.9) | non-fusion elementwise | flops 4194304 | bytes 25165824 | tf_op jit(solution)/shard_map/convert_element_type | solution.py:100
  151.6 12.3 %copy.97 = bf16[16,256,1024]{1,2,0:T(8,128)(2,1)} copy(bf16[16,256,1024]{2,1,0:T(8,128)(2,1)} %convert_element_type.87) | data formatting | bytes 16777216
  163.9 8.4 %pad.13.clone = bf16[16,256,1280]{1,2,0:T(8,128)(2,1)} pad(bf16[16,256,1024]{1,2,0:T(8,128)(2,1)} %copy.97, bf16[]{:T(256)} %constant.78.clone.1), padding=0_0x0_0x128_128 | pad | bytes 18874370 | tf_op jit(solution)/shard_map/jit(_pad)/pad | solution.py:57
  172.3 16.6 %fusion.48 = (bf16[16,256,8,128]{1,3,2,0:T(8,128)(2,1)}, bf16[16,256,8,128]{1,3,2,0:T(8,128)(2,1)}, bf16[16,256,8,128]{1,3,2,0:T(8,128)(2,1)}) fusion(bf16[16,256,10,128]{1,3,2,0:T(8,128)(2,1)} %bitcast.73), kind=kLoop, calls=%fused_computation.70 | loop fusion | bytes 50331648 | tf_op jit(solution)/shard_map/slice | solution.py:60
  188.9 11.4 %copy.94 = bf16[16,256,8,128]{3,1,0,2:T(8,128)(2,1)} copy(bf16[16,256,8,128]{1,3,2,0:T(8,128)(2,1)} %get-tuple-element.34) | data formatting | bytes 16777216
  200.4 11.4 %copy.95 = bf16[16,256,8,128]{3,1,0,2:T(8,128)(2,1)} copy(bf16[16,256,8,128]{1,3,2,0:T(8,128)(2,1)} %get-tuple-element.35) | data formatting | bytes 16777216
  211.7 11.4 %copy.96 = bf16[16,256,8,128]{3,1,0,2:T(8,128)(2,1)} copy(bf16[16,256,8,128]{1,3,2,0:T(8,128)(2,1)} %get-tuple-element.36) | data formatting | bytes 16777216
  223.1 12.4 %fusion = f32[256,8,128,1]{0,2,3,1:T(8,128)S(1)} fusion(bf16[16,256,8,128]{3,1,0,2:T(8,128)(2,1)} %copy.96, bf16[16,256,8,128]{3,1,0,2:T(8,128)(2,1)} %copy.95, bf16[16,256,8,128]{3,1,0,2:T(8,128)(2,1)} %copy.94, bf16[16,384,128]{1,2,0:T(8,128)(2,1)S(1)} %copy.73), kind=kOutput, calls=%fused_computation.1 | convolution fusion | flops 3296722944 | bytes 27787264 | tf_op jit(solution)/shard_map/krbp,kpq->rbq/dot_general | solution.py:101
  236.6 30.6 %all_to_all.33 = f32[1,256,1024]{1,0,2:T(1,128)S(1)} all-to-all(f32[1,256,1024]{1,0,2:T(1,128)S(1)} %copy.74), channel_id=1, replica_groups=mesh['exp'=8,'row'=4] {'exp'}, dimensions={2} | all-to-all | bytes 2097152 | tf_op jit(solution)/shard_map/all_to_all | solution.py:107
  (42 shorter events, 12.2 us)
Async XLA Ops:
  0.6 1.4 copy-start
  0.6 32.3 %copy-start.4 = (s32[1,256]{1,0:T(1,128)S(1)}, s32[1,256]{1,0:T(1,128)}, u32[]{:S(2)}) copy-start(s32[1,256]{1,0:T(1,128)} %param.17) | copy-start | bytes 3076
  3.6 21.8 %all-to-all-start = ((bf16[8,256,128]{2,1,0:T(8,128)(2,1)}), bf16[8,256,128]{2,1,0:T(8,128)(2,1)S(1)}, u32[]{:S(2)}, u32[]{:S(2)}) async-start(bf16[8,256,128]{2,1,0:T(8,128)(2,1)} %broadcast_select_fusion), calls=%async_computation | async-start | bytes 1048576 | tf_op jit(solution)/shard_map/all_to_all | solution.py:73
  25.6 8.6 %collective-permute-start.1 = (bf16[10,1024]{0,1:T(8,128)(2,1)S(1)}, bf16[10,1024]{0,1:T(8,128)(2,1)}, u32[]{:S(2)}, u32[]{:S(2)}) collective-permute-start(bf16[10,1024]{0,1:T(8,128)(2,1)S(1)} %bitcast.81), channel_id=1, source_target_pairs={{1,0},{2,1},{3,2},{5,4},{6,5},{7,6},{9,8},{10,9},{11,10},{13,12},{... | collective-permute-start | bytes 61448 | tf_op jit(solution)/shard_map/ppermute | solution.py:17
  26.9 7.1 %collective-permute-start = (bf16[10,1024]{1,0:T(8,128)(2,1)S(1)}, bf16[10,1024]{1,0:T(8,128)(2,1)S(1)}, u32[]{:S(2)}, u32[]{:S(2)}) collective-permute-start(bf16[10,1024]{1,0:T(8,128)(2,1)S(1)} %bitcast.84), channel_id=1, source_target_pairs={{0,1},{1,2},{2,3},{4,5},{5,6},{6,7},{8,9},{9,10},{10,11},{12,13},{... | collective-permute-start | bytes 61448 | tf_op jit(solution)/shard_map/ppermute | solution.py:15
  75.5 12.3 %copy-start.2 = (bf16[1,256,1024]{2,1,0:T(8,128)(2,1)S(1)}, bf16[1,256,1024]{2,1,0:T(8,128)(2,1)}, u32[]{:S(2)}) copy-start(bf16[1,256,1024]{2,1,0:T(8,128)(2,1)} %param.15) | copy-start | bytes 1572868
  88.9 24.1 %copy-start.3 = (bf16[16,21]{1,0:T(8,128)(2,1)S(1)}, bf16[16,21]{1,0:T(8,128)(2,1)}, u32[]{:S(2)}) copy-start(bf16[16,21]{1,0:T(8,128)(2,1)} %param.12) | copy-start | bytes 2020
  107.9 20.3 %collective-permute-start.2 = (bf16[16,10,1024]{2,1,0:T(8,128)(2,1)}, bf16[16,10,1024]{2,1,0:T(8,128)(2,1)}, u32[]{:S(2)}, u32[]{:S(2)}) collective-permute-start(bf16[16,10,1024]{2,1,0:T(8,128)(2,1)} %get-tuple-element.38), channel_id=1, source_target_pairs={{0,1},{1,2},{2,3},{4,5},{5,6},{6,7},{8,9},{9,10},{10,11},{12,13},{... | collective-permute-start | bytes 983048 | tf_op jit(solution)/shard_map/ppermute | solution.py:27
  111.7 24.2 %collective-permute-start.3 = (bf16[16,10,1024]{2,1,0:T(8,128)(2,1)}, bf16[16,10,1024]{2,1,0:T(8,128)(2,1)}, u32[]{:S(2)}, u32[]{:S(2)}) collective-permute-start(bf16[16,10,1024]{2,1,0:T(8,128)(2,1)} %get-tuple-element.37), channel_id=1, source_target_pairs={{1,0},{2,1},{3,2},{5,4},{6,5},{7,6},{9,8},{10,9},{11,10},{13,12},{... | collective-permute-start | bytes 983048 | tf_op jit(solution)/shard_map/ppermute | solution.py:27
  223.1 46.0 %copy-start.1 = (bf16[4,256,128]{2,1,0:T(8,128)(2,1)S(1)}, bf16[4,256,128]{2,1,0:T(8,128)(2,1)}, u32[]{:S(2)}) copy-start(bf16[4,256,128]{2,1,0:T(8,128)(2,1)} %param.11) | copy-start | bytes 786436
  235.5 32.2 %copy-start.5 = (s32[8,1]{0,1:T(1,128)S(1)}, s32[8,1]{0,1:T(1,128)}, u32[]{:S(2)}) copy-start(s32[8,1]{0,1:T(1,128)} %param.16) | copy-start | bytes 100
where the time goes:
time: 271 us; the launch traced here: 269 us
  local copies, waits for them, and re-layouts  133 us (49%)
  matrix products  58.5 us (22%)
  blocking collectives  30.6 us (11%)
  other arithmetic  17.5 us (6%)
  starting transfers between devices  16.7 us (6%)
  waiting for transfers between devices  12.1 us (4%)
    unnamed x23, local copies, waits for them, and re-layouts  52.9 us
    all_to_all x1, blocking collectives, body(): lax.all_to_all(own_term[None], 'exp', split_axis=2, concat_axis=0, tiled=...  30.6 us
    convert_element_type x2, local copies, waits for them, and re-layouts, body(): rowblur.reshape(kernel_count, strip_rows + 2 * halfwidth, cell_width)  22.3 us
    slice x2, local copies, waits for them, and re-layouts, stacked_blocks(): blocked[..., :-2, :]  18.2 us
    dot_general x1, matrix products, body(): jnp.einsum('kyi,kyx->kix', matrix, weighted, preferred_element_type=jnp.f...  16.5 us
    slice x1, local copies, waits for them, and re-layouts, body(): middle = colback_ext[:, halfwidth:strip_rows + halfwidth]  12.6 us
    dot_general x1, matrix products, body(): jnp.einsum('krbp,kpq->rbq', stacked_blocks(colback), bands(row_taps, True...  12.4 us
    dot_general x1, matrix products, body(): jnp.einsum('kyi,kix->kyx', matrix, rowblur, preferred_element_type=jnp.fl...  12.3 us
  transfers between devices with their start and end apart: 5, of which 1 were waited for; matrix products, arithmetic and copies ran while one was open for 11% of the time, Pallas kernels for 0%

commit v1 on v0

v1 whole, which is shorter than its diff:
```python
import functools

import jax
import jax.numpy as jnp
from jax import lax
from jax.experimental import pallas as pl
from jax.experimental.pallas import tpu as pltpu
from jax.sharding import PartitionSpec as P

LANES = 128
WINDOW = 256
PACK = 16
STEP = 64


def round_up(value, step):
    return -(-value // step) * step


def from_behind(block, axis, distance):
    devices = range(lax.axis_size(axis))
    route = [(i - distance, i) for i in devices if i - distance in devices]
    return lax.ppermute(block, axis, route)


def toeplitz(taps_row, rows, first):
    parts = []
    for at in range(0, rows, STEP):
        moved = pltpu.roll(jnp.broadcast_to(taps_row, (8, WINDOW)), (first + at) % WINDOW, 1)
        spread = jnp.broadcast_to(moved[:1], (min(STEP, rows - at), WINDOW))
        parts.append(pltpu.roll(spread, 0, 1, stride=1, stride_axis=0))
    return jnp.concatenate(parts, axis=0)


def filters_kernel(
    dims,
    lat_ref, taps_ref, obs_ref, mask_ref, coef_hbm, above_hbm, below_hbm,
    res_ref, term_ref,
    coef, lsh, fw, gw, aw, bw, rb, resid, cb, tsh, sems,
):
    kernels, tap_count, strip, width, inner, outer = dims
    half_width = tap_count // 2
    half = strip // 2
    block = half + inner
    chunks = width // WINDOW

    def copies(c):
        cols = pl.ds(c * WINDOW, WINDOW)
        return (
            pltpu.make_async_copy(
                coef_hbm.at[:, :, cols], coef.at[:, pl.ds(inner, strip), cols], sems.at[c, 0]),
            pltpu.make_async_copy(
                above_hbm.at[:, :, cols], coef.at[:, pl.ds(0, inner), cols], sems.at[c, 1]),
            pltpu.make_async_copy(
                below_hbm.at[:, :, cols], coef.at[:, pl.ds(inner + strip, inner), cols], sems.at[c, 2]),
        )

    for c in range(chunks):
        for copy in copies(c):
            copy.start()

    lsh[:, pl.ds(0, LANES)] = jnp.zeros((lsh.shape[0], LANES), lsh.dtype)
    lsh[:, pl.ds(width, LANES)] = jnp.zeros((lsh.shape[0], LANES), lsh.dtype)
    lsh[:, pl.ds(LANES // 2, width)] = lat_ref[...]

    low_a = strip + 2 * outer - WINDOW
    low_b = strip + 2 * inner - WINDOW
    side = LANES // 2 + half_width

    @pl.loop(0, kernels // 2)
    def _(pair):
        for odd in range(2):
            k = 2 * pair + odd
            row = taps_ref[0, pl.ds(k, 1), :]
            row_rev = taps_ref[1, pl.ds(k, 1), :]
            col = taps_ref[2, pl.ds(k, 1), :]
            col_rev = taps_ref[3, pl.ds(k, 1), :]
            shape = (pl.ds(odd * LANES, LANES))
            fw[pair, :, shape] = toeplitz(row_rev, WINDOW, -side)[:, :LANES].astype(fw.dtype)
            gw[k] = toeplitz(row, WINDOW, -side)[:, :LANES].astype(gw.dtype)
            aw[k, 0] = toeplitz(col, block, outer - inner - half_width).astype(aw.dtype)
            aw[k, 1] = toeplitz(col, block, half + outer - half_width - low_a).astype(aw.dtype)
            bw[k, 0] = toeplitz(col_rev, half, inner - half_width).astype(bw.dtype)
            bw[k, 1] = toeplitz(col_rev, half, half + inner - half_width - low_b).astype(bw.dtype)

    @pl.loop(0, chunks)
    def _(c):
        for copy in copies(c):
            copy.wait()
        start = pl.multiple_of(c * WINDOW, WINDOW)
        cols = pl.ds(start, WINDOW)
        for b in range(WINDOW // LANES):
            window = lsh[:, pl.ds(pl.multiple_of(start + b * LANES, LANES), WINDOW)]
            for pair in range(kernels // 2):
                both = jnp.dot(window, fw[pair], preferred_element_type=jnp.float32).astype(rb.dtype)
                rb[2 * pair, :, pl.ds(b * LANES, LANES)] = both[:, :LANES]
                rb[2 * pair + 1, :, pl.ds(b * LANES, LANES)] = both[:, LANES:]
        for part in range(2):
            rows = pl.ds(part * block, block)
            seen = pl.ds(part * low_a, WINDOW)
            predicted = jnp.zeros((block, WINDOW), jnp.float32)
            for k in range(kernels):
                vertical = jnp.dot(aw[k, part], rb[k, seen, :], preferred_element_type=jnp.float32)
                predicted += coef[k, rows, cols].astype(jnp.float32) * vertical
            mask = mask_ref[rows, :]
            mask = jnp.concatenate([mask] * (WINDOW // LANES), axis=1)
            resid[rows, :] = mask * (predicted - obs_ref[rows, cols].astype(jnp.float32))
        res_ref[:, cols] = resid[pl.ds(inner, strip), :]
        for k in range(kernels):
            weighted = (coef[k, :, cols].astype(jnp.float32) * resid[...]).astype(jnp.bfloat16)
            for part in range(2):
                seen = weighted[part * low_b:part * low_b + WINDOW]
                back = jnp.dot(bw[k, part], seen, preferred_element_type=jnp.float32)
                cb[k, pl.ds(part * half, half), cols] = back.astype(cb.dtype)

    blocks = width // LANES
    for out, source, taps_at in (
        (0, 0, LANES), (width, width - LANES, 0),
    ):
        total = jnp.zeros((strip, LANES), jnp.float32)
        for k in range(kernels):
            total += jnp.dot(
                cb[k, :, pl.ds(source, LANES)], gw[k, pl.ds(taps_at, LANES), :],
                preferred_element_type=jnp.float32)
        tsh[:, pl.ds(out, LANES)] = total

    @pl.loop(0, blocks - 1)
    def _(b):
        source = pl.multiple_of(b * LANES, LANES)
        total = jnp.zeros((strip, LANES), jnp.float32)
        for k in range(kernels):
            total += jnp.dot(
                cb[k, :, pl.ds(source, WINDOW)], gw[k], preferred_element_type=jnp.float32)
        tsh[:, pl.ds(pl.multiple_of(source + LANES, LANES), LANES)] = total

    term_ref[...] = tsh[:, pl.ds(LANES // 2, width)].astype(term_ref.dtype)


def body(latent, row_taps, column_taps, coefficients, observed, cell_of, valid_rows):
    kernels, tap_count = row_taps.shape
    half_width = tap_count // 2
    strip, width = observed.shape[1:]
    ncells = latent.shape[0]
    inner = round_up(half_width, PACK)
    outer = round_up(2 * half_width, PACK)
    cell_list = cell_of[:, 0]

    above_coef = from_behind(coefficients[0, :, strip - inner:], "row", 1)
    below_coef = from_behind(coefficients[0, :, :inner], "row", -1)
    usable = jnp.broadcast_to(valid_rows[0].astype(jnp.bfloat16)[:, None], (strip, LANES))
    seen = jnp.concatenate([observed[0], usable], axis=1)
    seen = jnp.concatenate(
        [from_behind(seen[strip - inner:], "row", 1), seen, from_behind(seen[:inner], "row", -1)], axis=0)
    mask = seen[:, width:].astype(jnp.float32)
    seen = seen[:, :width]

    outgoing = jnp.take(latent, cell_list, axis=0)
    arrived = lax.all_to_all(outgoing, "exp", split_axis=0, concat_axis=2, tiled=True)[0]
    extended = jnp.concatenate(
        [from_behind(arrived[strip - outer:], "row", 1), arrived, from_behind(arrived[:outer], "row", -1)], axis=0)

    taps = jnp.stack([row_taps, row_taps[:, ::-1], column_taps, column_taps[:, ::-1]]).astype(jnp.float32)
    taps = jnp.pad(taps, ((0, 0), (0, 0), (0, WINDOW - tap_count)))

    vmem = pl.BlockSpec(memory_space=pltpu.VMEM)
    hbm = pl.BlockSpec(memory_space=pl.ANY)
    dims = (kernels, tap_count, strip, width, inner, outer)
    block = strip // 2 + inner
    bf16 = jnp.bfloat16
    residual, term = pl.pallas_call(
        functools.partial(filters_kernel, dims),
        out_shape=(
            jax.ShapeDtypeStruct((strip, width), jnp.float32),
            jax.ShapeDtypeStruct((strip, width), bf16),
        ),
        in_specs=[vmem, vmem, vmem, vmem, hbm, hbm, hbm],
        out_specs=(vmem, vmem),
        scratch_shapes=[
            pltpu.VMEM((kernels, strip + 2 * inner, width), bf16),
            pltpu.VMEM((strip + 2 * outer, width + LANES), bf16),
            pltpu.VMEM((kernels // 2, WINDOW, 2 * LANES), bf16),
            pltpu.VMEM((kernels, WINDOW, LANES), bf16),
            pltpu.VMEM((kernels, 2, block, WINDOW), bf16),
            pltpu.VMEM((kernels, 2, strip // 2, WINDOW), bf16),
            pltpu.VMEM((kernels, strip + 2 * outer, WINDOW), bf16),
            pltpu.VMEM((strip + 2 * inner, WINDOW), jnp.float32),
            pltpu.VMEM((kernels, strip, width), bf16),
            pltpu.VMEM((strip, width + LANES), jnp.float32),
            pltpu.SemaphoreType.DMA((width // WINDOW, 3)),
        ],
        compiler_params=pltpu.CompilerParams(vmem_limit_bytes=56 * 2**20),
        cost_estimate=pl.CostEstimate(flops=10**10, bytes_accessed=2 * 10**7, transcendentals=0),
    )(extended, taps, seen, mask, coefficients[0], above_coef, below_coef)

    incoming = lax.all_to_all(term[None], "exp", split_axis=2, concat_axis=0, tiled=True)
    owner = jnp.arange(ncells)[:, None] == cell_list[None, :]
    gradient = jnp.sum(
        jnp.where(owner[:, :, None, None], incoming[None].astype(jnp.float32), 0.0), axis=1)
    return (gradient, residual[None])


def solution(mesh):
    placed = (
        P(None, "row", "exp"),
        P(),
        P(),
        P("exp", None, "row", None),
        P("exp", "row", None),
        P(),
        P("exp", "row"),
    )
    return jax.shard_map(
        body,
        mesh=mesh,
        in_specs=placed,
        out_specs=(P(None, "row", "exp"), P("exp", "row", None)),
        check_vma=False,
    )
```

time: 271 us -> 94.8 us (0.35)
  local copies, waits for them, and re-layouts: 133 us -> 9.45 us
  matrix products: 58.5 us -> 0 us
  blocking collectives: 30.6 us -> 0 us
  Pallas kernels: 0 us -> 28.4 us
  starting transfers between devices: 16.7 us -> 24.9 us
  other arithmetic: 17.5 us -> 10.7 us
  waiting for transfers between devices: 12.1 us -> 18.8 us
    dot_general x8 -> x0, matrix products: 58.5 us -> none  [the longest x1 16.5 us: body(): jnp.einsum('kyi,kyx->kix', matrix, weighted, preferred_element_type=jnp.f...]
    unnamed x23 -> x20, local copies, waits for them, and re-layouts: 52.9 us -> 2.9 us
    slice x7 -> x4, local copies, waits for them, and re-layouts: 33.3 us -> 0.97 us  [the longest x1 0.9 us: body(): seen = seen[:, :width]]
    all_to_all x1 -> x0, blocking collectives: 30.6 us -> none  [body(): lax.all_to_all(own_term[None], 'exp', split_axis=2, concat_axis=0, tiled=...]
    pallas_call x0 -> x1, Pallas kernels: none -> 28.4 us  [body(): pl.pallas_call(functools.partial(filters_kernel, dims), out_shape=(jax.Sh...]
    convert_element_type x3 -> x1, local copies, waits for them, and re-layouts: 23.8 us -> 0.64 us  [body(): incoming[None].astype(jnp.float32)]
    scatter-add x2 -> x0, local copies, waits for them, and re-layouts: 11.1 us -> none  [the longest x1 5.94 us: body(): middle = middle.at[:, :halfwidth].add(from_above)]
    pad x1 -> x0, local copies, waits for them, and re-layouts: 8.39 us -> none  [stacked_blocks(): padded = jnp.pad(source, padding)]
  transfers between devices with their start and end apart: 5 -> 8, of which waited for: 1 -> 3; matrix products, arithmetic and copies ran while one was open for 11% -> 6% of each run, Pallas kernels for 0% -> 0%
where the time goes in v1:
time: 94.8 us; the launch traced here: 93.1 us
  Pallas kernels  28.4 us (30%)
  starting transfers between devices  24.9 us (26%)
  waiting for transfers between devices  18.8 us (20%)
  other arithmetic  10.7 us (11%)
  local copies, waits for them, and re-layouts  9.45 us (10%)
    pallas_call x1, Pallas kernels, body(): pl.pallas_call(functools.partial(filters_kernel, dims), out_shape=(jax.Sh...  28.4 us
    all_to_all x1, waiting for transfers between devices, body(): lax.all_to_all(term[None], 'exp', split_axis=2, concat_axis=0, tiled=True)  14.2 us
    ppermute x6, starting transfers between devices, from_behind(): return lax.ppermute(block, axis, route)  11.7 us
    all_to_all x1, starting transfers between devices, body(): lax.all_to_all(outgoing, 'exp', split_axis=0, concat_axis=2, tiled=True)[0]  7.28 us
    all_to_all x1, starting transfers between devices, body(): lax.all_to_all(term[None], 'exp', split_axis=2, concat_axis=0, tiled=True)  5.92 us
    unnamed x1, other arithmetic  3.82 us
    unnamed x20, local copies, waits for them, and re-layouts  2.9 us
    all_to_all x1, waiting for transfers between devices, body(): lax.all_to_all(outgoing, 'exp', split_axis=0, concat_axis=2, tiled=True)[0]  2.54 us
  transfers between devices with their start and end apart: 8, of which 3 were waited for; matrix products, arithmetic and copies ran while one was open for 6% of the time, Pallas kernels for 0%

profile of v1, /device:TPU:0, one launch (start us, length us, event | category | flops | bytes accessed | tf_op | source)
XLA Modules:
  0.0 93.1 jit_solution(226902734414984991)
XLA Ops:
  0.6 0.7 fusion.8
  1.3 0.7 and_bitcast_fusion
  2.0 0.6 gather_fusion
  2.7 0.9 broadcast_select_fusion
  3.6 7.3 %all-to-all-start = ((bf16[8,256,128]{2,1,0:T(8,128)(2,1)}), bf16[8,256,128]{2,1,0:T(8,128)(2,1)S(1)}, u32[]{:S(2)}, u32[]{:S(2)}) async-start(bf16[8,256,128]{2,1,0:T(8,128)(2,1)} %broadcast_select_fusion), calls=%async_computation | async-start | bytes 1048576 | tf_op jit(solution)/shard_map/all_to_all | solution.py:158
  10.9 0.1 broadcast_in_dim.48
  11.1 1.5 %collective-permute-start.2 = (bf16[16,1152]{1,0:T(8,128)(2,1)S(1)}, bf16[16,1152]{1,0:T(8,128)(2,1)S(1)}, u32[]{:S(2)}, u32[]{:S(2)}) collective-permute-start(bf16[16,1152]{1,0:T(8,128)(2,1)S(1)} %get-tuple-element.8), channel_id=1, source_target_pairs={{0,1},{1,2},{2,3},{4,5},{5,6},{6,7},{8,9},{9,10},{10,11},{12,13},{... | collective-permute-start | bytes 110600 | tf_op jit(solution)/shard_map/ppermute | solution.py:23
  12.5 1.3 %collective-permute-start.3 = (bf16[16,1152]{1,0:T(8,128)(2,1)S(1)}, bf16[16,1152]{1,0:T(8,128)(2,1)S(1)}, u32[]{:S(2)}, u32[]{:S(2)}) collective-permute-start(bf16[16,1152]{1,0:T(8,128)(2,1)S(1)} %get-tuple-element.9), channel_id=1, source_target_pairs={{1,0},{2,1},{3,2},{5,4},{6,5},{7,6},{9,8},{10,9},{11,10},{13,12},{... | collective-permute-start | bytes 110600 | tf_op jit(solution)/shard_map/ppermute | solution.py:23
  13.8 1.3 %slice_bitcast_fusion = (bf16[16,16,1024]{2,1,0:T(8,128)(2,1)S(1)}, bf16[16,16,1024]{2,1,0:T(8,128)(2,1)S(1)}) fusion(bf16[1,16,256,1024]{3,2,1,0:T(8,128)(2,1)} %param.10), kind=kLoop, calls=%fused_computation.6 | loop fusion | bytes 2097152 | tf_op jit(solution)/shard_map/squeeze | solution.py:149
  15.1 4.6 %collective-permute-start.4 = (bf16[16,16,1024]{2,1,0:T(8,128)(2,1)S(1)}, bf16[16,16,1024]{2,1,0:T(8,128)(2,1)S(1)}, u32[]{:S(2)}, u32[]{:S(2)}) collective-permute-start(bf16[16,16,1024]{2,1,0:T(8,128)(2,1)S(1)} %get-tuple-element.7), channel_id=1, source_target_pairs={{0,1},{1,2},{2,3},{4,5},{5,6},{6,7},{8,9},{9,10},{10,11},{12,13},{... | collective-permute-start | bytes 1572872 | tf_op jit(solution)/shard_map/ppermute | solution.py:23
  19.8 1.3 %collective-permute-start.5 = (bf16[16,16,1024]{2,1,0:T(8,128)(2,1)S(1)}, bf16[16,16,1024]{2,1,0:T(8,128)(2,1)}, u32[]{:S(2)}, u32[]{:S(2)}) collective-permute-start(bf16[16,16,1024]{2,1,0:T(8,128)(2,1)S(1)} %get-tuple-element.6), channel_id=1, source_target_pairs={{1,0},{2,1},{3,2},{5,4},{6,5},{7,6},{9,8},{10,9},{11,10},{13,12},{... | collective-permute-start | bytes 1572872 | tf_op jit(solution)/shard_map/ppermute | solution.py:23
  21.3 0.6 fusion.7.taps_ref
  21.9 0.9 slice.44.obs_ref
  22.8 2.5 %all-to-all-done = bf16[8,256,128]{2,1,0:T(8,128)(2,1)S(1)} async-done(((bf16[8,256,128]{2,1,0:T(8,128)(2,1)}), bf16[8,256,128]{2,1,0:T(8,128)(2,1)S(1)}, u32[]{:S(2)}, u32[]{:S(2)}) %all-to-all-start) | async-done | bytes 524320 | tf_op jit(solution)/shard_map/all_to_all | solution.py:158
  25.5 1.7 %collective-permute-start = (bf16[32,1024]{1,0:T(8,128)(2,1)S(1)}, bf16[32,1024]{1,0:T(8,128)(2,1)S(1)}, u32[]{:S(2)}, u32[]{:S(2)}) collective-permute-start(bf16[32,1024]{1,0:T(8,128)(2,1)S(1)} %bitcast.56), channel_id=1, source_target_pairs={{0,1},{1,2},{2,3},{4,5},{5,6},{6,7},{8,9},{9,10},{10,11},{12,13},{... | collective-permute-start | bytes 196616 | tf_op jit(solution)/shard_map/ppermute | solution.py:23
  27.2 1.3 %collective-permute-start.1 = (bf16[32,1024]{1,0:T(8,128)(2,1)S(1)}, bf16[32,1024]{1,0:T(8,128)(2,1)S(1)}, u32[]{:S(2)}, u32[]{:S(2)}) collective-permute-start(bf16[32,1024]{1,0:T(8,128)(2,1)S(1)} %bitcast.57), channel_id=1, source_target_pairs={{1,0},{2,1},{3,2},{5,4},{6,5},{7,6},{9,8},{10,9},{11,10},{13,12},{... | collective-permute-start | bytes 196616 | tf_op jit(solution)/shard_map/ppermute | solution.py:23
  28.5 0.7 maximum_convert_fusion.mask_ref
  29.2 0.3 copy.19
  29.7 2.0 %collective-permute-done.1 = bf16[32,1024]{1,0:T(8,128)(2,1)S(1)} collective-permute-done((bf16[32,1024]{1,0:T(8,128)(2,1)S(1)}, bf16[32,1024]{1,0:T(8,128)(2,1)S(1)}, u32[]{:S(2)}, u32[]{:S(2)}) %collective-permute-start.1) | collective-permute-done | bytes 65568 | tf_op jit(solution)/shard_map/ppermute | solution.py:23
  31.7 0.9 pad_maximum_fusion.1.lat_ref
  32.6 0.8 copy-done.4
  33.4 28.4 %shard_map.86 = (f32[256,1024]{1,0:T(8,128)}, bf16[256,1024]{1,0:T(8,128)(2,1)}) custom-call(bf16[320,1024]{1,0:T(8,128)(2,1)} %pad_maximum_fusion.1.lat_ref, f32[4,16,256]{2,1,0:T(8,128)} %fusion.7.taps_ref, bf16[288,1024]{1,0:T(8,128)(2,1)} %slice.44.obs_ref, f32[288,128]{1,0:T(8,128)} %maximum_convert_fusion.mask_ref, bf16[16,256,1024]{2,1,0:T(8,128)(2,1)} %bitcast.55, ...), custom_call_target="tpu_custom_call" | custom-call | flops 10000000000 | bytes 20000000 | tf_op jit(solution)/shard_map/pallas_call | solution.py:170
  61.8 2.4 %copy.21 = bf16[1,256,1024]{1,0,2:T(2,128)(2,1)S(1)} copy(bf16[1,256,1024]{2,1,0:T(8,128)(2,1)} %bitcast.52) | data formatting | bytes 1048576 | tf_op jit(solution)/shard_map/broadcast_in_dim | solution.py:195
  64.2 0.5 broadcast.43
  64.7 3.8 %reduce.2 = bf16[1024,256]{1,0:T(8,128)(2,1)S(1)} reduce(bf16[1024,1,256]{2,1,0:T(2,128)(2,1)S(1)} %bitcast.45, bf16[]{:T(256)} %broadcast.43), dimensions={1}, to_apply=%bitcast.37.reduce_sub_computation | reduce | bytes 1048578
  68.6 0.9 reshape.60
  69.5 5.9 %all-to-all-start.1 = ((bf16[8,2,16384]{2,1,0:T(2,128)(2,1)}), bf16[8,2,16384]{2,1,0:T(2,128)(2,1)S(1)}, u32[]{:S(2)}, u32[]{:S(2)}) async-start(bf16[8,2,16384]{2,1,0:T(2,128)(2,1)} %reshape.60), calls=%async_computation.1 | async-start | bytes 1048576 | tf_op jit(solution)/shard_map/all_to_all | solution.py:195
  75.4 14.2 %all-to-all-done.1 = bf16[8,2,16384]{2,1,0:T(2,128)(2,1)S(1)} async-done(((bf16[8,2,16384]{2,1,0:T(2,128)(2,1)}), bf16[8,2,16384]{2,1,0:T(2,128)(2,1)S(1)}, u32[]{:S(2)}, u32[]{:S(2)}) %all-to-all-start.1) | async-done | bytes 524320 | tf_op jit(solution)/shard_map/all_to_all | solution.py:195
  89.6 0.5 reshape.61
  90.1 1.1 %convert_bitcast_fusion = f32[8,1,256,128]{2,1,3,0:T(1,128)S(1)} fusion(bf16[1,256,8,128]{1,0,3,2:T(2,128)(2,1)S(1)} %bitcast.47), kind=kLoop, calls=%fused_computation.2 | loop fusion | flops 262144 | bytes 1572864 | tf_op jit(solution)/shard_map/convert_element_type | solution.py:198
  91.2 0.6 copy.23
  91.9 1.3 %select_reduce_fusion = f32[4,256,128]{2,1,0:T(8,128)} fusion(f32[8,256,128]{2,1,0:T(8,128)S(1)} %bitcast.46, pred[4,8]{1,0:T(4,128)(4,1)S(1)} %iota_compare_fusion.1), kind=kLoop, calls=%fused_computation.1 | loop fusion | flops 1966080 | bytes 1572896 | tf_op jit(solution)/shard_map/reduce_sum | solution.py:197
  (31 shorter events, 0.5 us)
Async XLA Ops:
  0.6 1.4 %copy-start = (bf16[4,256,128]{2,1,0:T(8,128)(2,1)S(1)}, bf16[4,256,128]{2,1,0:T(8,128)(2,1)}, u32[]{:S(2)}) copy-start(bf16[4,256,128]{2,1,0:T(8,128)(2,1)} %param.7) | copy-start | bytes 786436
  2.0 8.9 %copy-start.5 = (s32[1,256]{1,0:T(1,128)S(1)}, s32[1,256]{1,0:T(1,128)}, u32[]{:S(2)}) copy-start(s32[1,256]{1,0:T(1,128)} %param.13) | copy-start | bytes 3076
  2.7 8.3 %copy-start.1 = (bf16[1,256,1024]{2,1,0:T(8,128)(2,1)S(1)}, bf16[1,256,1024]{2,1,0:T(8,128)(2,1)}, u32[]{:S(2)}) copy-start(bf16[1,256,1024]{2,1,0:T(8,128)(2,1)} %param.11) | copy-start | bytes 1572868
  3.6 21.8 %all-to-all-start = ((bf16[8,256,128]{2,1,0:T(8,128)(2,1)}), bf16[8,256,128]{2,1,0:T(8,128)(2,1)S(1)}, u32[]{:S(2)}, u32[]{:S(2)}) async-start(bf16[8,256,128]{2,1,0:T(8,128)(2,1)} %broadcast_select_fusion), calls=%async_computation | async-start | bytes 1048576 | tf_op jit(solution)/shard_map/all_to_all | solution.py:158
  11.0 10.0 %copy-start.3 = (bf16[16,21]{1,0:T(8,128)(2,1)S(1)}, bf16[16,21]{1,0:T(8,128)(2,1)}, u32[]{:S(2)}) copy-start(bf16[16,21]{1,0:T(8,128)(2,1)} %param.8) | copy-start | bytes 2020
  11.1 10.1 %copy-start.2 = (bf16[16,21]{1,0:T(8,128)(2,1)S(1)}, bf16[16,21]{1,0:T(8,128)(2,1)}, u32[]{:S(2)}) copy-start(bf16[16,21]{1,0:T(8,128)(2,1)} %param.9) | copy-start | bytes 2020
  11.1 10.8 %collective-permute-start.2 = (bf16[16,1152]{1,0:T(8,128)(2,1)S(1)}, bf16[16,1152]{1,0:T(8,128)(2,1)S(1)}, u32[]{:S(2)}, u32[]{:S(2)}) collective-permute-start(bf16[16,1152]{1,0:T(8,128)(2,1)S(1)} %get-tuple-element.8), channel_id=1, source_target_pairs={{0,1},{1,2},{2,3},{4,5},{5,6},{6,7},{8,9},{9,10},{10,11},{12,13},{... | collective-permute-start | bytes 110600 | tf_op jit(solution)/shard_map/ppermute | solution.py:23
  12.5 9.3 %collective-permute-start.3 = (bf16[16,1152]{1,0:T(8,128)(2,1)S(1)}, bf16[16,1152]{1,0:T(8,128)(2,1)S(1)}, u32[]{:S(2)}, u32[]{:S(2)}) collective-permute-start(bf16[16,1152]{1,0:T(8,128)(2,1)S(1)} %get-tuple-element.9), channel_id=1, source_target_pairs={{1,0},{2,1},{3,2},{5,4},{6,5},{7,6},{9,8},{10,9},{11,10},{13,12},{... | collective-permute-start | bytes 110600 | tf_op jit(solution)/shard_map/ppermute | solution.py:23
  15.1 17.4 %collective-permute-start.4 = (bf16[16,16,1024]{2,1,0:T(8,128)(2,1)S(1)}, bf16[16,16,1024]{2,1,0:T(8,128)(2,1)S(1)}, u32[]{:S(2)}, u32[]{:S(2)}) collective-permute-start(bf16[16,16,1024]{2,1,0:T(8,128)(2,1)S(1)} %get-tuple-element.7), channel_id=1, source_target_pairs={{0,1},{1,2},{2,3},{4,5},{5,6},{6,7},{8,9},{9,10},{10,11},{12,13},{... | collective-permute-start | bytes 1572872 | tf_op jit(solution)/shard_map/ppermute | solution.py:23
  19.8 12.8 %collective-permute-start.5 = (bf16[16,16,1024]{2,1,0:T(8,128)(2,1)S(1)}, bf16[16,16,1024]{2,1,0:T(8,128)(2,1)}, u32[]{:S(2)}, u32[]{:S(2)}) collective-permute-start(bf16[16,16,1024]{2,1,0:T(8,128)(2,1)S(1)} %get-tuple-element.6), channel_id=1, source_target_pairs={{1,0},{2,1},{3,2},{5,4},{6,5},{7,6},{9,8},{10,9},{11,10},{13,12},{... | collective-permute-start | bytes 1572872 | tf_op jit(solution)/shard_map/ppermute | solution.py:23
  25.5 4.2 %collective-permute-start = (bf16[32,1024]{1,0:T(8,128)(2,1)S(1)}, bf16[32,1024]{1,0:T(8,128)(2,1)S(1)}, u32[]{:S(2)}, u32[]{:S(2)}) collective-permute-start(bf16[32,1024]{1,0:T(8,128)(2,1)S(1)} %bitcast.56), channel_id=1, source_target_pairs={{0,1},{1,2},{2,3},{4,5},{5,6},{6,7},{8,9},{9,10},{10,11},{12,13},{... | collective-permute-start | bytes 196616 | tf_op jit(solution)/shard_map/ppermute | solution.py:23
  27.2 4.5 %collective-permute-start.1 = (bf16[32,1024]{1,0:T(8,128)(2,1)S(1)}, bf16[32,1024]{1,0:T(8,128)(2,1)S(1)}, u32[]{:S(2)}, u32[]{:S(2)}) collective-permute-start(bf16[32,1024]{1,0:T(8,128)(2,1)S(1)} %bitcast.57), channel_id=1, source_target_pairs={{1,0},{2,1},{3,2},{5,4},{6,5},{7,6},{9,8},{10,9},{11,10},{13,12},{... | collective-permute-start | bytes 196616 | tf_op jit(solution)/shard_map/ppermute | solution.py:23
  32.6 0.8 copy-start.4
  68.6 6.8 %copy-start.6 = (s32[8,1]{0,1:T(1,128)S(1)}, s32[8,1]{0,1:T(1,128)}, u32[]{:S(2)}) copy-start(s32[8,1]{0,1:T(1,128)} %param.12) | copy-start | bytes 100
  69.5 20.1 %all-to-all-start.1 = ((bf16[8,2,16384]{2,1,0:T(2,128)(2,1)}), bf16[8,2,16384]{2,1,0:T(2,128)(2,1)S(1)}, u32[]{:S(2)}, u32[]{:S(2)}) async-start(bf16[8,2,16384]{2,1,0:T(2,128)(2,1)} %reshape.60), calls=%async_computation.1 | async-start | bytes 1048576 | tf_op jit(solution)/shard_map/all_to_all | solution.py:195

commit v2 on v1

--- a/solution.py
+++ b/solution.py
@@ -11,6 +11,7 @@
 WINDOW = 256
 PACK = 16
 STEP = 64
+MESH = pl.DeviceIdType.MESH
 
 
 def round_up(value, step):
@@ -136,7 +137,7 @@
     term_ref[...] = tsh[:, pl.ds(LANES // 2, width)].astype(term_ref.dtype)
 
 
-def body(latent, row_taps, column_taps, coefficients, observed, cell_of, valid_rows):
+def apart_body(latent, row_taps, column_taps, coefficients, observed, cell_of, valid_rows):
     kernels, tap_count = row_taps.shape
     half_width = tap_count // 2
     strip, width = observed.shape[1:]
@@ -199,6 +200,367 @@
     return (gradient, residual[None])
 
 
+def fused_kernel(
+    dims,
+    cells_ref, lat_ref, taps_ref, obs_hbm, use_hbm, coef_hbm,
+    res_ref, grad_ref,
+    coef, seen, usable, outgoing, lat, lsh, fw, gw, aw, bw, rb, resid, cb, tsh, leaving, arrived,
+    own_sems, lat_send, lat_recv, rim_send, rim_recv, halo_send, halo_recv, term_send, term_recv,
+):
+    count, row_count, kernels, tap_count, strip, width, inner, outer = dims
+    half_width = tap_count // 2
+    half = strip // 2
+    block = half + inner
+    chunks = width // WINDOW
+    per = WINDOW // LANES
+    me = lax.axis_index("exp")
+    row = lax.axis_index("row")
+    rising = me < count // 2
+    has_above = row > 0
+    has_below = row < row_count - 1
+
+    def ordered(rank, length):
+        return jnp.where(rising, rank, length - 1 - rank)
+
+    def reversed_order(rank, length):
+        return jnp.where(rising, length - 1 - rank, rank)
+
+    def lane_block(b):
+        return pl.ds(pl.multiple_of(b * LANES, LANES), LANES)
+
+    def chunk_cols(c):
+        return pl.ds(pl.multiple_of(c * WINDOW, WINDOW), WINDOW)
+
+    barrier = pltpu.get_barrier_semaphore()
+    for e in range(count):
+        @pl.when(e != me)
+        def _():
+            pl.semaphore_signal(barrier, inc=1, device_id={"exp": e}, device_id_type=MESH)
+
+    @pl.when(has_above)
+    def _():
+        pl.semaphore_signal(barrier, inc=1, device_id={"row": row - 1}, device_id_type=MESH)
+
+    @pl.when(has_below)
+    def _():
+        pl.semaphore_signal(barrier, inc=1, device_id={"row": row + 1}, device_id_type=MESH)
+
+    def own_coef(c):
+        cols = chunk_cols(c)
+        return pltpu.make_async_copy(
+            coef_hbm.at[:, :, cols], coef.at[:, pl.ds(inner, strip), cols], own_sems.at[c])
+
+    own_seen = pltpu.make_async_copy(obs_hbm, seen.at[pl.ds(inner, strip)], own_sems.at[chunks])
+    own_use = pltpu.make_async_copy(use_hbm, usable.at[pl.ds(inner, strip)], own_sems.at[chunks + 1])
+    own_seen.start()
+    own_use.start()
+    for step in range(chunks):
+        own_coef(ordered(step, chunks)).start()
+
+    for e in range(count):
+        outgoing[e] = lat_ref[cells_ref[e, 0]]
+    for ref in (lat,):
+        ref[:, pl.ds(0, LANES)] = jnp.zeros((ref.shape[0], LANES), ref.dtype)
+        ref[:, pl.ds(LANES + width, LANES)] = jnp.zeros((ref.shape[0], LANES), ref.dtype)
+
+    def fill(at_lat, at_inner):
+        lat[pl.ds(at_lat, outer), :] = jnp.zeros((outer, lat.shape[1]), lat.dtype)
+        coef[:, pl.ds(at_inner, inner), :] = jnp.zeros((kernels, inner, width), coef.dtype)
+        seen[pl.ds(at_inner, inner), :] = jnp.zeros((inner, width), seen.dtype)
+        usable[pl.ds(at_inner, inner), :] = jnp.zeros((inner, LANES), usable.dtype)
+
+    @pl.when(jnp.logical_not(has_above))
+    def _():
+        fill(0, 0)
+
+    @pl.when(jnp.logical_not(has_below))
+    def _():
+        fill(outer + strip, inner + strip)
+
+    pl.semaphore_wait(barrier, count - 1 + has_above.astype(jnp.int32) + has_below.astype(jnp.int32))
+
+    strip_rows = pl.ds(outer, strip)
+
+    def lat_copy(e):
+        return pltpu.make_async_remote_copy(
+            src_ref=outgoing.at[e], dst_ref=lat.at[strip_rows, lane_block(me + 1)],
+            send_sem=lat_send.at[e], recv_sem=lat_recv.at[me],
+            device_id={"exp": e}, device_id_type=MESH)
+
+    def own_lat():
+        return pltpu.make_async_copy(
+            outgoing.at[me], lat.at[strip_rows, lane_block(me + 1)], lat_recv.at[me])
+
+    def halo_copies(c, side):
+        cols = chunk_cols(c)
+        source = pl.ds(0 if side == 0 else strip - inner, inner)
+        target = pl.ds(inner + strip if side == 0 else 0, inner)
+        return pltpu.make_async_remote_copy(
+            src_ref=coef_hbm.at[:, source, cols], dst_ref=coef.at[:, target, cols],
+            send_sem=halo_send.at[side, c], recv_sem=halo_recv.at[side, c],
+            device_id={"row": row - 1 if side == 0 else row + 1}, device_id_type=MESH)
+
+    def seen_copies(side):
+        source = pl.ds(0 if side == 0 else strip - inner, inner)
+        target = pl.ds(inner + strip if side == 0 else 0, inner)
+        return [pltpu.make_async_remote_copy(
+            src_ref=src.at[source], dst_ref=dst.at[target],
+            send_sem=halo_send.at[side, chunks + i], recv_sem=halo_recv.at[side, chunks + i],
+            device_id={"row": row - 1 if side == 0 else row + 1}, device_id_type=MESH)
+            for i, (src, dst) in enumerate(((obs_hbm, seen), (use_hbm, usable)))]
+
+    def rim_copy(b, side):
+        cols = lane_block(b + 1)
+        source = pl.ds(outer if side == 0 else strip, outer)
+        target = pl.ds(outer + strip if side == 0 else 0, outer)
+        return pltpu.make_async_remote_copy(
+            src_ref=lat.at[source, cols], dst_ref=lat.at[target, cols],
+            send_sem=rim_send.at[side, b], recv_sem=rim_recv.at[side, b],
+            device_id={"row": row - 1 if side == 0 else row + 1}, device_id_type=MESH)
+
+    sends = ((0, has_above), (1, has_below))
+    receives = ((0, has_below), (1, has_above))
+
+    own_lat().start()
+    for rank in range(count):
+        e = ordered(rank, count)
+        @pl.when(e != me)
+        def _():
+            lat_copy(e).start()
+    for side, there in sends:
+        @pl.when(there)
+        def _():
+            for copy in seen_copies(side):
+                copy.start()
+            for step in range(chunks):
+                halo_copies(ordered(step, chunks), side).start()
+
+    low_a = strip + 2 * outer - WINDOW
+    low_b = strip + 2 * inner - WINDOW
+    shift = LANES // 2 + half_width
+
+    @pl.loop(0, kernels // 2)
+    def _(pair):
+        for odd in range(2):
+            k = 2 * pair + odd
+            along = taps_ref[0, pl.ds(k, 1), :]
+            along_rev = taps_ref[1, pl.ds(k, 1), :]
+            down = taps_ref[2, pl.ds(k, 1), :]
+            down_rev = taps_ref[3, pl.ds(k, 1), :]
+            fw[pair, :, pl.ds(odd * LANES, LANES)] = toeplitz(along_rev, WINDOW, -shift)[:, :LANES].astype(fw.dtype)
+            gw[k] = toeplitz(along, WINDOW, -shift)[:, :LANES].astype(gw.dtype)
+            aw[k, 0] = toeplitz(down, block, outer - inner - half_width).astype(aw.dtype)
+            aw[k, 1] = toeplitz(down, block, half + outer - half_width - low_a).astype(aw.dtype)
+            bw[k, 0] = toeplitz(down_rev, half, inner - half_width).astype(bw.dtype)
+            bw[k, 1] = toeplitz(down_rev, half, half + inner - half_width - low_b).astype(bw.dtype)
+
+    for at in (0, LANES + width):
+        cb[:, :, pl.ds(at, LANES)] = jnp.zeros((kernels, strip, LANES), cb.dtype)
+
+    def take_block(rank):
+        b = ordered(rank, count)
+        pltpu.make_async_copy(
+            outgoing.at[0], lat.at[strip_rows, lane_block(b + 1)], lat_recv.at[b]).wait()
+        for side, there in sends:
+            @pl.when(there)
+            def _():
+                rim_copy(b, side).start()
+
+    def take_rims(rank):
+        b = ordered(rank, count)
+        for side, there in receives:
+            @pl.when(there)
+            def _():
+                rim_copy(b, side).wait_recv()
+
+    for rank in range(per + 1):
+        take_block(rank)
+    own_seen.wait()
+    own_use.wait()
+    for side, there in receives:
+        @pl.when(there)
+        def _():
+            for copy in seen_copies(side):
+                copy.wait_recv()
+    take_rims(0)
+
+    @pl.loop(0, chunks)
+    def _(step):
+        c = ordered(step, chunks)
+        cols = chunk_cols(c)
+        for more in range(1, per + 1):
+            @pl.when(step * per + more < count)
+            def _():
+                take_rims(step * per + more)
+        near = lat[:, pl.ds(pl.multiple_of(c * WINDOW, WINDOW), WINDOW + 2 * LANES)]
+        lsh[...] = near[:, LANES // 2:LANES // 2 + WINDOW + LANES]
+        for b in range(per):
+            window = lsh[:, pl.ds(b * LANES, WINDOW)]
+            for pair in range(kernels // 2):
+                both = jnp.dot(window, fw[pair], preferred_element_type=jnp.float32).astype(rb.dtype)
+                rb[2 * pair, :, pl.ds(b * LANES, LANES)] = both[:, :LANES]
+                rb[2 * pair + 1, :, pl.ds(b * LANES, LANES)] = both[:, LANES:]
+        own_coef(c).wait()
+        for side, there in receives:
+            @pl.when(there)
+            def _():
+                halo_copies(c, side).wait_recv()
+        for part in range(2):
+            if part == 1:
+                for more in range(1, per + 1):
+                    @pl.when((step + 1) * per + more < count)
+                    def _():
+                        take_block((step + 1) * per + more)
+            rows = pl.ds(part * block, block)
+            reach = pl.ds(part * low_a, WINDOW)
+            predicted = jnp.zeros((block, WINDOW), jnp.float32)
+            for k in range(kernels):
+                vertical = jnp.dot(aw[k, part], rb[k, reach, :], preferred_element_type=jnp.float32)
+                predicted += coef[k, rows, cols].astype(jnp.float32) * vertical
+            mask = usable[rows, :].astype(jnp.float32)
+            mask = jnp.concatenate([mask] * per, axis=1)
+            resid[rows, cols] = mask * (predicted - seen[rows, cols].astype(jnp.float32))
+        res_ref[:, cols] = resid[pl.ds(inner, strip), cols]
+
+    def term_copy(b):
+        return pltpu.make_async_remote_copy(
+            src_ref=leaving.at[b], dst_ref=arrived.at[me],
+            send_sem=term_send.at[b], recv_sem=term_recv.at[me],
+            device_id={"exp": b}, device_id_type=MESH)
+
+    def window_sum(rank):
+        m = reversed_order(rank, count + 1)
+        reach = pl.ds(pl.multiple_of(m * LANES, LANES), WINDOW)
+        total = jnp.zeros((strip, LANES), jnp.float32)
+        for k in range(kernels):
+            total += jnp.dot(cb[k, :, reach], gw[k], preferred_element_type=jnp.float32)
+        tsh[:, lane_block(m)] = total
+
+    def send_term(rank):
+        b = reversed_order(rank, count)
+        both = tsh[:, pl.ds(pl.multiple_of(b * LANES, LANES), WINDOW)]
+        leaving[b] = both[:, LANES // 2:LANES // 2 + LANES].astype(leaving.dtype)
+
+        @pl.when(b != me)
+        def _():
+            term_copy(b).start()
+
+    @pl.loop(0, chunks)
+    def _(step):
+        c = reversed_order(step, chunks)
+        cols = chunk_cols(c)
+        ahead = pl.ds(pl.multiple_of(c * WINDOW + LANES, LANES), WINDOW)
+        for k in range(kernels):
+            weighted = (coef[k, :, cols].astype(jnp.float32) * resid[:, cols]).astype(jnp.bfloat16)
+            for part in range(2):
+                reach = weighted[part * low_b:part * low_b + WINDOW]
+                back = jnp.dot(bw[k, part], reach, preferred_element_type=jnp.float32)
+                cb[k, pl.ds(part * half, half), ahead] = back.astype(cb.dtype)
+
+        @pl.loop(step * per, step * per + per)
+        def _(rank):
+            window_sum(rank)
+
+            @pl.when(rank > 0)
+            def _():
+                send_term(rank - 1)
+
+    window_sum(count)
+    send_term(count - 1)
+
+    for c in range(grad_ref.shape[0]):
+        mine = (cells_ref[me, 0] == c).astype(jnp.float32)
+        grad_ref[c] = mine * leaving[me].astype(jnp.float32)
+    for rank in range(count):
+        e = reversed_order(rank, count)
+
+        @pl.when(e != me)
+        def _():
+            pltpu.make_async_copy(leaving.at[0], arrived.at[e], term_recv.at[e]).wait()
+            value = arrived[e].astype(jnp.float32)
+            for c in range(grad_ref.shape[0]):
+                grad_ref[c] += (cells_ref[e, 0] == c).astype(jnp.float32) * value
+
+    for e in range(count):
+        @pl.when(e != me)
+        def _():
+            lat_copy(e).wait_send()
+            term_copy(e).wait_send()
+    for side, there in sends:
+        @pl.when(there)
+        def _():
+            for copy in seen_copies(side):
+                copy.wait_send()
+            for c in range(chunks):
+                halo_copies(c, side).wait_send()
+            for b in range(count):
+                rim_copy(b, side).wait_send()
+
+
+def fused_body(latent, row_taps, column_taps, coefficients, observed, cell_of, valid_rows):
+    kernels, tap_count = row_taps.shape
+    half_width = tap_count // 2
+    strip, width = observed.shape[1:]
+    ncells = latent.shape[0]
+    inner = round_up(half_width, PACK)
+    outer = round_up(2 * half_width, PACK)
+    count, row_count = lax.axis_size("exp"), lax.axis_size("row")
+    usable = jnp.broadcast_to(valid_rows[0].astype(jnp.bfloat16)[:, None], (strip, LANES))
+    taps = jnp.stack([row_taps, row_taps[:, ::-1], column_taps, column_taps[:, ::-1]]).astype(jnp.float32)
+    taps = jnp.pad(taps, ((0, 0), (0, 0), (0, WINDOW - tap_count)))
+
+    vmem = pl.BlockSpec(memory_space=pltpu.VMEM)
+    smem = pl.BlockSpec(memory_space=pltpu.SMEM)
+    hbm = pl.BlockSpec(memory_space=pl.ANY)
+    chunks = width // WINDOW
+    block = strip // 2 + inner
+    bf16 = jnp.bfloat16
+    dma = pltpu.SemaphoreType.DMA
+    dims = (count, row_count, kernels, tap_count, strip, width, inner, outer)
+    residual, gradient = pl.pallas_call(
+        functools.partial(fused_kernel, dims),
+        out_shape=(
+            jax.ShapeDtypeStruct((strip, width), jnp.float32),
+            jax.ShapeDtypeStruct((ncells, strip, LANES), jnp.float32),
+        ),
+        in_specs=[smem, vmem, vmem, hbm, hbm, hbm],
+        out_specs=(vmem, vmem),
+        scratch_shapes=[
+            pltpu.VMEM((kernels, strip + 2 * inner, width), bf16),
+            pltpu.VMEM((strip + 2 * inner, width), bf16),
+            pltpu.VMEM((strip + 2 * inner, LANES), bf16),
+            pltpu.VMEM((count, strip, LANES), bf16),
+            pltpu.VMEM((strip + 2 * outer, width + 2 * LANES), bf16),
+            pltpu.VMEM((strip + 2 * outer, WINDOW + LANES), bf16),
+            pltpu.VMEM((kernels // 2, WINDOW, 2 * LANES), bf16),
+            pltpu.VMEM((kernels, WINDOW, LANES), bf16),
+            pltpu.VMEM((kernels, 2, block, WINDOW), bf16),
+            pltpu.VMEM((kernels, 2, strip // 2, WINDOW), bf16),
+            pltpu.VMEM((kernels, strip + 2 * outer, WINDOW), bf16),
+            pltpu.VMEM((strip + 2 * inner, width), jnp.float32),
+            pltpu.VMEM((kernels, strip, width + 2 * LANES), bf16),
+            pltpu.VMEM((strip, width + LANES), jnp.float32),
+            pltpu.VMEM((count, strip, LANES), bf16),
+            pltpu.VMEM((count, strip, LANES), bf16),
+            dma((chunks + 2,)),
+            dma((count,)), dma((count,)),
+            dma((2, count)), dma((2, count)),
+            dma((2, chunks + 2)), dma((2, chunks + 2)),
+            dma((count,)), dma((count,)),
+        ],
+        compiler_params=pltpu.CompilerParams(
+            vmem_limit_bytes=56 * 2**20, collective_id=0, has_side_effects=True),
+        cost_estimate=pl.CostEstimate(flops=10**10, bytes_accessed=2 * 10**7, transcendentals=0),
+    )(cell_of, latent, taps, observed[0], usable, coefficients[0])
+    return (gradient, residual[None])
+
+
+def body(latent, *others):
+    if latent.shape[2] == LANES:
+        return fused_body(latent, *others)
+    return apart_body(latent, *others)
+
+
 def solution(mesh):
     placed = (
         P(None, "row", "exp"),

time: 94.8 us -> 61.1 us (0.64); the launches traced: 93.1 us -> 60.7 us
  starting transfers between devices: 24.9 us -> 0 us
  Pallas kernels: 28.4 us -> 50.3 us
  waiting for transfers between devices: 18.8 us -> 0 us
  other arithmetic: 10.7 us -> 2.04 us
  local copies, waits for them, and re-layouts: 9.45 us -> 7.76 us
    pallas_call x1, Pallas kernels: 28.4 us -> 50.3 us  [fused_body(): pl.pallas_call(functools.partial(fused_kernel, dims), out_shape=(jax.Shap...]
    all_to_all x2 -> x0, waiting for transfers between devices: 16.7 us -> none  [the longest x1 14.2 us: body(): lax.all_to_all(term[None], 'exp', split_axis=2, concat_axis=0, tiled=True)]
    all_to_all x2 -> x0, starting transfers between devices: 13.2 us -> none  [the longest x1 7.28 us: body(): lax.all_to_all(outgoing, 'exp', split_axis=0, concat_axis=2, tiled=True)[0]]
    ppermute x6 -> x0, starting transfers between devices: 11.7 us -> none  [from_behind(): return lax.ppermute(block, axis, route)]
    unnamed x1 -> x0, other arithmetic: 3.82 us -> none
    unnamed x20 -> x3, local copies, waits for them, and re-layouts: 2.9 us -> 5.49 us
    ppermute x6 -> x0, waiting for transfers between devices: 2.04 us -> none  [from_behind(): return lax.ppermute(block, axis, route)]
    broadcast_in_dim x2 -> x1, local copies, waits for them, and re-layouts: 2.5 us -> 0.73 us  [fused_body(): jnp.broadcast_to(valid_rows[0].astype(jnp.bfloat16)[:, None], (strip, LAN...]
  transfers between devices with their start and end apart: 8 -> 0, of which waited for: 3 -> 0; matrix products, arithmetic and copies ran while one was open for 6% -> 0% of each run, Pallas kernels for 0% -> 0%
where the time goes in v2:
time: 61.1 us; the launch traced here: 60.7 us
  Pallas kernels  50.3 us (82%)
  local copies, waits for them, and re-layouts  7.76 us (13%)
  other arithmetic  2.04 us (3%)
  between operations  0.64 us (1%)
    pallas_call x1, Pallas kernels, fused_body(): pl.pallas_call(functools.partial(fused_kernel, dims), out_shape=(jax.Shap...  50.3 us
    unnamed x3, local copies, waits for them, and re-layouts  5.49 us
    pad x1, other arithmetic, fused_body(): taps = jnp.pad(taps, ((0, 0), (0, 0), (0, WINDOW - tap_count)))  1.34 us

profile of v2, /device:TPU:0, one launch (start us, length us, event | category | flops | bytes accessed | tf_op | source)
XLA Modules:
  0.0 60.7 jit_solution(18106539877566792279)
XLA Ops:
  0.6 0.7 %convert_reduce_fusion = bf16[256]{0:T(256)(128)(2,1)S(1)} fusion(s32[1,256]{1,0:T(1,128)} %param.13), kind=kLoop, calls=%fused_computation.9 | loop fusion | flops 256 | bytes 1536 | tf_op jit(solution)/shard_map/convert_element_type | solution.py:508
  1.3 1.3 %copy.9.cells_ref = s32[8,1]{1,0:T(8,128)} copy(s32[8,1]{0,1:T(1,128)} %param.12) | data formatting | bytes 64 | tf_op args[5]
  2.6 0.8 %rev.6 = bf16[16,21]{1,0:T(8,128)(2,1)S(1)} reverse(bf16[16,21]{1,0:T(8,128)(2,1)} %param.8), dimensions={1} | reverse | bytes 1344 | tf_op jit(solution)/shard_map/rev | solution.py:509
  3.4 0.8 %rev.7 = bf16[16,21]{1,0:T(8,128)(2,1)S(1)} reverse(bf16[16,21]{1,0:T(8,128)(2,1)} %param.9), dimensions={1} | reverse | bytes 1344 | tf_op jit(solution)/shard_map/rev | solution.py:509
  4.2 1.3 %fusion.7.taps_ref = f32[4,16,256]{2,1,0:T(8,128)} fusion(bf16[1,16,21]{2,1,0:T(8,128)(2,1)S(1)} %bitcast.11, bf16[1,16,21]{2,1,0:T(8,128)(2,1)} %bitcast.8, bf16[1,16,21]{2,1,0:T(8,128)(2,1)S(1)} %bitcast.10, bf16[1,16,21]{2,1,0:T(8,128)(2,1)} %bitcast.9), kind=kLoop, calls=%fused_computation.8 | loop fusion | flops 212992 | bytes 68224 | tf_op jit(solution)/shard_map/jit(_pad)/pad | solution.py:510
  5.5 0.7 %broadcast_in_dim.4.use_hbm = bf16[256,128]{1,0:T(8,128)(2,1)} broadcast(bf16[256]{0:T(256)(128)(2,1)S(1)} %convert_reduce_fusion), dimensions={0} | broadcast | bytes 66048 | tf_op jit(solution)/shard_map/broadcast_in_dim | solution.py:508
  6.3 50.3 %shard_map.86 = (f32[256,1024]{1,0:T(8,128)}, f32[4,256,128]{2,1,0:T(8,128)}) custom-call(s32[8,1]{1,0:T(8,128)} %copy.9.cells_ref, bf16[4,256,128]{2,1,0:T(8,128)(2,1)} %lat_ref.1, f32[4,16,256]{2,1,0:T(8,128)} %fusion.7.taps_ref, bf16[256,1024]{1,0:T(8,128)(2,1)} %bitcast.13, bf16[256,128]{1,0:T(8,128)(2,1)} %broadcast_in_dim.4.use_hbm, ...), custom_call_target="tpu_custom_call" | custom-call | flops 10000000000 | bytes 20000000 | tf_op jit(solution)/shard_map/pallas_call | solution.py:520
  56.5 1.9 %copy.12 = f32[4,256,128]{2,1,0:T(8,128)} copy(f32[4,256,128]{2,1,0:T(8,128)} %get-tuple-element.8) | data formatting | bytes 1048576
  58.4 2.3 %copy.13 = f32[1,256,1024]{2,1,0:T(8,128)} copy(f32[1,256,1024]{2,1,0:T(8,128)} %bitcast.7) | data formatting | bytes 2097152
